TPU v7x, 512 devices: a whole 4x4x16 slice. The times are simulated.
512 devices in a mesh: au: 16 (over x_hi, y, core), vert: 32 (over z, x_lo).
Axes of the slice: x: 4 (x_hi: 2, x_lo: 2; x = x_hi * 2 + x_lo), y: 4, z: 16, core: 2. Of those that a mesh axis runs over, the one named last changes fastest.
Arguments:
- views: bfloat16 [32, 16, 16, 4096], P('vert', 'au'), may hold values from -6 to 6
- shifts: int32 [32, 16, 32], P('vert', 'au'), may hold values from -16 to 16
Outputs:
- refined: float32 [32, 16, 16, 4096], P('vert', None, 'au')
All inputs are finite; a program needn't handle non-finite values.
Results may differ from a plain program's by a relative error of at most 0.0003.
Values may be sent and summed in bfloat16 or wider, within the bound.
A program may use at most 64 MiB of HBM per device.

v0:
```python
import jax
import jax.numpy as jnp
from jax import lax
from jax.sharding import PartitionSpec as P

MAXS = 16
RAD = 2


def partner(block, axis, stride):
    count = lax.axis_size(axis)
    route = []
    for low in range(count):
        high = low | 1 << stride
        if high != low and high < count:
            route += [(low, high), (high, low)]
    return lax.ppermute(block, axis, route)


def label_costs(band, mirror, shift_row):
    width = band.shape[1]
    own = jnp.pad(band.astype(jnp.float32), ((0, 0), (MAXS, MAXS)))
    other = jnp.pad(mirror.astype(jnp.float32), ((0, 0), (MAXS, MAXS)))
    sheared = []
    for offset in range(-MAXS, MAXS + 1):
        moved = own[:, MAXS + offset : MAXS + offset + width]
        facing = other[:, MAXS - offset : MAXS - offset + width]
        sheared.append((moved - facing) ** 2)
    squares = jnp.stack(sheared, axis=0)
    padded = jnp.pad(squares, ((0, 0), (0, 0), (RAD, RAD)))
    total = padded[:, :, 0:width]
    for offset in range(1, 2 * RAD + 1):
        total = total + padded[:, :, offset : offset + width]
    candidates = jnp.arange(-MAXS, MAXS + 1, dtype=jnp.int32)
    select = (shift_row[:, None] == candidates[None, :]).astype(jnp.float32)
    return jnp.einsum(
        "ls,srw->lrw",
        select,
        total,
        precision=lax.Precision.HIGHEST,
        preferred_element_type=jnp.float32,
    )


def soft_depth(cost, label_axis):
    scores = -0.5 * cost
    weight = jax.nn.softmax(scores, axis=label_axis)
    count = cost.shape[label_axis]
    shape = [1] * cost.ndim
    shape[label_axis] = count
    labels = jnp.arange(count, dtype=jnp.float32).reshape(shape)
    depth = jnp.sum(weight * labels, axis=label_axis)
    confidence = jnp.max(weight, axis=label_axis)
    return (depth, confidence)


def refine_epi(intens, depth, confidence):
    cams, rows, width = intens.shape
    padx = jnp.pad(intens, ((0, 0), (0, 0), (1, 1)))
    grad_x = 0.5 * (padx[:, :, 2:] - padx[:, :, :-2])
    padu = jnp.pad(intens, ((1, 1), (0, 0), (0, 0)))
    grad_u = 0.5 * (padu[2:] - padu[:-2])

    def boxed(field):
        padded = jnp.pad(field, ((1, 1), (0, 0), (RAD, RAD)))
        total = jnp.zeros((cams, rows, width), jnp.float32)
        for du in range(3):
            for dx in range(2 * RAD + 1):
                total = total + padded[du : du + cams, :, dx : dx + width]
        return total

    jxx = boxed(grad_x * grad_x)
    jxu = boxed(grad_x * grad_u)
    slope = -jxu / (jxx + 1.0)
    coherence = jxx / (jxx + 1.0)
    return (confidence * depth + 4.0 * coherence * slope) / (confidence + coherence)


def column_mirror(block):
    for bit in range(lax.axis_size("au").bit_length() - 1):
        block = partner(block, "au", bit)
    return block


def row_mirror(block):
    for bit in range(1, lax.axis_size("vert").bit_length() - 1):
        block = partner(block, "vert", bit)
    return block


def local(views, shifts):
    band = views[0, 0]
    mirror = column_mirror(row_mirror(band))
    cost = label_costs(band, mirror, shifts[0, 0])
    intens = lax.all_to_all(band[None, None], "au", split_axis=2, concat_axis=0, tiled=True)[
        :, 0
    ].astype(jnp.float32)
    gathered = lax.all_to_all(cost[None], "au", split_axis=2, concat_axis=0, tiled=True)
    depth, confidence = soft_depth(gathered, 1)
    return refine_epi(intens, depth, confidence)[None]


def solution(mesh):
    placed = (P("vert", "au", None, None), P("vert", "au", None))
    return jax.shard_map(
        local, mesh=mesh, in_specs=placed, out_specs=P("vert", None, "au", None), check_vma=False
    )
```

profile of v0, /device:TPU:27, one launch (start us, length us, event | category | flops | bytes accessed | tf_op | source)
XLA Modules:
  0.0 329.2 jit_solution(1068889963009563014)
XLA Ops:
  0.0 3.7 %collective-permute-start = (bf16[16,4096]{1,0:T(8,128)(2,1)}, bf16[16,4096]{1,0:T(8,128)(2,1)S(1)}, u32[]{:S(2)}, u32[]{:S(2)}) collective-permute-start(bf16[16,4096]{1,0:T(8,128)(2,1)} %bitcast.104), channel_id=1, source_target_pairs={{0,2},{2,0},{1,3},{3,1},{4,6},{6,4},{5,7},{7,5},{8,10},{10,8},{9,1... | collective-permute-start | bytes 393224 | tf_op jit(solution)/shard_map/ppermute | solution.py:17
  3.7 3.3 %collective-permute-done = bf16[16,4096]{1,0:T(8,128)(2,1)S(1)} collective-permute-done((bf16[16,4096]{1,0:T(8,128)(2,1)}, bf16[16,4096]{1,0:T(8,128)(2,1)S(1)}, u32[]{:S(2)}, u32[]{:S(2)}) %collective-permute-start) | collective-permute-done | bytes 131104 | tf_op jit(solution)/shard_map/ppermute | solution.py:17
  7.0 4.9 %collective-permute-start.1 = (bf16[16,4096]{1,0:T(8,128)(2,1)S(1)}, bf16[16,4096]{1,0:T(8,128)(2,1)S(1)}, u32[]{:S(2)}, u32[]{:S(2)}) collective-permute-start(bf16[16,4096]{1,0:T(8,128)(2,1)S(1)} %collective-permute-done), channel_id=1, source_target_pairs={{0,4},{4,0},{1,5},{5,1},{2,6},{6,2},{3,7},{7,3},{8,12},{12,8},{9,1... | collective-permute-start | bytes 393224 | tf_op jit(solution)/shard_map/ppermute | solution.py:17
  11.9 5.7 %collective-permute-done.1 = bf16[16,4096]{1,0:T(8,128)(2,1)S(1)} collective-permute-done((bf16[16,4096]{1,0:T(8,128)(2,1)S(1)}, bf16[16,4096]{1,0:T(8,128)(2,1)S(1)}, u32[]{:S(2)}, u32[]{:S(2)}) %collective-permute-start.1) | collective-permute-done | bytes 131104 | tf_op jit(solution)/shard_map/ppermute | solution.py:17
  17.6 8.8 %collective-permute-start.2 = (bf16[16,4096]{1,0:T(8,128)(2,1)S(1)}, bf16[16,4096]{1,0:T(8,128)(2,1)S(1)}, u32[]{:S(2)}, u32[]{:S(2)}) collective-permute-start(bf16[16,4096]{1,0:T(8,128)(2,1)S(1)} %collective-permute-done.1), channel_id=1, source_target_pairs={{0,8},{8,0},{1,9},{9,1},{2,10},{10,2},{3,11},{11,3},{4,12},{12,4},... | collective-permute-start | bytes 393224 | tf_op jit(solution)/shard_map/ppermute | solution.py:17
  26.4 10.7 %collective-permute-done.2 = bf16[16,4096]{1,0:T(8,128)(2,1)S(1)} collective-permute-done((bf16[16,4096]{1,0:T(8,128)(2,1)S(1)}, bf16[16,4096]{1,0:T(8,128)(2,1)S(1)}, u32[]{:S(2)}, u32[]{:S(2)}) %collective-permute-start.2) | collective-permute-done | bytes 131104 | tf_op jit(solution)/shard_map/ppermute | solution.py:17
  37.1 13.6 %collective-permute-start.3 = (bf16[16,4096]{1,0:T(8,128)(2,1)S(1)}, bf16[16,4096]{1,0:T(8,128)(2,1)S(1)}, u32[]{:S(2)}, u32[]{:S(2)}) collective-permute-start(bf16[16,4096]{1,0:T(8,128)(2,1)S(1)} %collective-permute-done.2), channel_id=1, source_target_pairs={{0,16},{16,0},{1,17},{17,1},{2,18},{18,2},{3,19},{19,3},{4,20},{20... | collective-permute-start | bytes 393224 | tf_op jit(solution)/shard_map/ppermute | solution.py:17
  50.7 11.7 %collective-permute-done.3 = bf16[16,4096]{1,0:T(8,128)(2,1)S(1)} collective-permute-done((bf16[16,4096]{1,0:T(8,128)(2,1)S(1)}, bf16[16,4096]{1,0:T(8,128)(2,1)S(1)}, u32[]{:S(2)}, u32[]{:S(2)}) %collective-permute-start.3) | collective-permute-done | bytes 131104 | tf_op jit(solution)/shard_map/ppermute | solution.py:17
  62.4 2.9 collective-permute-start.4
  66.3 2.4 collective-permute-start.5
  68.7 4.2 %collective-permute-done.5 = bf16[16,4096]{1,0:T(8,128)(2,1)S(1)} collective-permute-done((bf16[16,4096]{1,0:T(8,128)(2,1)S(1)}, bf16[16,4096]{1,0:T(8,128)(2,1)S(1)}, u32[]{:S(2)}, u32[]{:S(2)}) %collective-permute-start.5) | collective-permute-done | bytes 131104 | tf_op jit(solution)/shard_map/ppermute | solution.py:17
  72.9 2.9 collective-permute-start.6
  79.5 7.2 %all-to-all-start.1 = ((bf16[16,2,2048]{2,1,0:T(2,128)(2,1)}), bf16[16,2,2048]{2,1,0:T(2,128)(2,1)S(1)}, u32[]{:S(2)}, u32[]{:S(2)}) async-start(bf16[16,2,2048]{2,1,0:T(2,128)(2,1)} %reshape.98), calls=%async_computation.1 | async-start | bytes 262144 | tf_op jit(solution)/shard_map/all_to_all | solution.py:95
  86.7 4.6 %collective-permute-start.7 = (bf16[16,4096]{1,0:T(8,128)(2,1)S(1)}, bf16[16,4096]{1,0:T(8,128)(2,1)S(1)}, u32[]{:S(2)}, u32[]{:S(2)}) collective-permute-start(bf16[16,4096]{1,0:T(8,128)(2,1)S(1)} %collective-permute-done.6), channel_id=1, source_target_pairs={{0,256},{256,0},{32,288},{288,32},{64,320},{320,64},{96,352},{352,... | collective-permute-start | bytes 393224 | tf_op jit(solution)/shard_map/ppermute | solution.py:17
  92.3 2.6 collective-permute-done.7
  124.8 21.5 %slice_add_fusion = f32[33,16,4096]{2,1,0:T(8,128)} fusion(f32[33,16,4096]{2,1,0:T(8,128)} %bitcast_dynamic-update-slice_fusion), kind=kLoop, calls=%fused_computation.2 | loop fusion | flops 8650752 | bytes 17301504 | tf_op jit(solution)/shard_map/add | solution.py:33
  146.3 16.2 %fusion.5 = f32[1,32,16,4096]{3,1,0,2:T(8,128)} fusion(f32[33,16,4096]{2,1,0:T(8,128)} %slice_add_fusion, s32[33]{0:T(128)S(1)} %iota_add_fusion, s32[32]{0:T(128)S(1)} %bitcast.106), kind=kOutput, calls=%fused_computation.10 | convolution fusion | flops 830473216 | bytes 17039620 | tf_op jit(solution)/shard_map/ls,srw->lrw/dot_general | solution.py:36
  162.5 8.1 %all-to-all-start = ((f32[1,32,16,4096]{3,1,0,2:T(8,128)}), f32[1,32,16,4096]{3,1,0,2:T(8,128)}, u32[]{:S(2)}, u32[]{:S(2)}) async-start(f32[1,32,16,4096]{3,1,0,2:T(8,128)} %fusion.5), calls=%async_computation | async-start | bytes 16777216 | tf_op jit(solution)/shard_map/all_to_all | solution.py:98
  170.9 2.2 fusion.15
  173.2 126.4 %all-to-all-done = f32[1,32,16,4096]{3,1,0,2:T(8,128)} async-done(((f32[1,32,16,4096]{3,1,0,2:T(8,128)}), f32[1,32,16,4096]{3,1,0,2:T(8,128)}, u32[]{:S(2)}, u32[]{:S(2)}) %all-to-all-start) | async-done | bytes 8388640 | tf_op jit(solution)/shard_map/all_to_all | solution.py:98
  299.6 4.7 %bitcast_reduce_fusion = f32[16,4096]{1,0:T(8,128)S(1)} fusion(f32[1,32,16,4096]{3,1,0,2:T(8,128)} %all-to-all-done), kind=kLoop, calls=%fused_computation.6 | loop fusion | flops 4128768 | bytes 8650752 | tf_op jit(solution)/shard_map/reduce_max | solution.py:47
  304.3 5.2 %fusion.4 = f32[16,4096]{1,0:T(8,128)S(1)} fusion(f32[1,32,16,4096]{3,1,0,2:T(8,128)} %all-to-all-done, f32[16,4096]{1,0:T(8,128)S(1)} %bitcast_reduce_fusion), kind=kLoop, calls=%fused_computation.9 | loop fusion | flops 6225920 | bytes 8912896 | tf_op jit(solution)/shard_map/reduce_sum | solution.py:47
  309.6 5.3 %fusion.8 = (f32[16,4096]{1,0:T(8,128)S(1)}, f32[16,4096]{1,0:T(8,128)S(1)}) fusion(f32[16,4096]{1,0:T(8,128)S(1)} %fusion.4, f32[16,4096]{1,0:T(8,128)S(1)} %bitcast_reduce_fusion, f32[1,32,16,4096]{3,1,0,2:T(8,128)} %all-to-all-done), kind=kLoop, calls=%fused_computation.11 | loop fusion | flops 12451840 | bytes 9437184 | tf_op jit(solution)/shard_map/reduce_max | solution.py:53
  314.9 14.3 %fusion.10 = f32[1,16,1,4096]{3,2,1,0:T(1,128)} fusion(f32[16,1,4096]{2,1,0:T(1,128)S(1)} %get-tuple-element.8, f32[16,1,4096]{2,1,0:T(1,128)S(1)} %get-tuple-element.7, f32[16,4096]{1,0:T(8,128)S(1)} %get-tuple-element.6, f32[16,4096]{1,0:T(8,128)S(1)} %get-tuple-element.5), kind=kLoop, calls=%fused_computation.54 | loop fusion | flops 2490368 | bytes 1310720 | tf_op jit(solution)/shard_map/broadcast_in_dim | solution.py:100
  (49 shorter events, 36.0 us)
Async XLA Ops:
  0.0 109.5 %copy-start = (bf16[1,1,16,4096]{3,2,1,0:T(8,128)(2,1)S(1)}, bf16[1,1,16,4096]{3,2,1,0:T(8,128)(2,1)}, u32[]{:S(2)}) copy-start(bf16[1,1,16,4096]{3,2,1,0:T(8,128)(2,1)} %param.2) | copy-start | bytes 393220
  0.0 7.0 %collective-permute-start = (bf16[16,4096]{1,0:T(8,128)(2,1)}, bf16[16,4096]{1,0:T(8,128)(2,1)S(1)}, u32[]{:S(2)}, u32[]{:S(2)}) collective-permute-start(bf16[16,4096]{1,0:T(8,128)(2,1)} %bitcast.104), channel_id=1, source_target_pairs={{0,2},{2,0},{1,3},{3,1},{4,6},{6,4},{5,7},{7,5},{8,10},{10,8},{9,1... | collective-permute-start | bytes 393224 | tf_op jit(solution)/shard_map/ppermute | solution.py:17
  7.0 10.6 %collective-permute-start.1 = (bf16[16,4096]{1,0:T(8,128)(2,1)S(1)}, bf16[16,4096]{1,0:T(8,128)(2,1)S(1)}, u32[]{:S(2)}, u32[]{:S(2)}) collective-permute-start(bf16[16,4096]{1,0:T(8,128)(2,1)S(1)} %collective-permute-done), channel_id=1, source_target_pairs={{0,4},{4,0},{1,5},{5,1},{2,6},{6,2},{3,7},{7,3},{8,12},{12,8},{9,1... | collective-permute-start | bytes 393224 | tf_op jit(solution)/shard_map/ppermute | solution.py:17
  17.6 19.5 %collective-permute-start.2 = (bf16[16,4096]{1,0:T(8,128)(2,1)S(1)}, bf16[16,4096]{1,0:T(8,128)(2,1)S(1)}, u32[]{:S(2)}, u32[]{:S(2)}) collective-permute-start(bf16[16,4096]{1,0:T(8,128)(2,1)S(1)} %collective-permute-done.1), channel_id=1, source_target_pairs={{0,8},{8,0},{1,9},{9,1},{2,10},{10,2},{3,11},{11,3},{4,12},{12,4},... | collective-permute-start | bytes 393224 | tf_op jit(solution)/shard_map/ppermute | solution.py:17
  37.1 25.3 %collective-permute-start.3 = (bf16[16,4096]{1,0:T(8,128)(2,1)S(1)}, bf16[16,4096]{1,0:T(8,128)(2,1)S(1)}, u32[]{:S(2)}, u32[]{:S(2)}) collective-permute-start(bf16[16,4096]{1,0:T(8,128)(2,1)S(1)} %collective-permute-done.2), channel_id=1, source_target_pairs={{0,16},{16,0},{1,17},{17,1},{2,18},{18,2},{3,19},{19,3},{4,20},{20... | collective-permute-start | bytes 393224 | tf_op jit(solution)/shard_map/ppermute | solution.py:17
  62.4 3.9 %collective-permute-start.4 = (bf16[16,4096]{1,0:T(8,128)(2,1)S(1)}, bf16[16,4096]{1,0:T(8,128)(2,1)S(1)}, u32[]{:S(2)}, u32[]{:S(2)}) collective-permute-start(bf16[16,4096]{1,0:T(8,128)(2,1)S(1)} %collective-permute-done.3), channel_id=1, source_target_pairs={{0,32},{32,0},{64,96},{96,64},{128,160},{160,128},{192,224},{224,1... | collective-permute-start | bytes 393224 | tf_op jit(solution)/shard_map/ppermute | solution.py:17
  66.3 6.6 %collective-permute-start.5 = (bf16[16,4096]{1,0:T(8,128)(2,1)S(1)}, bf16[16,4096]{1,0:T(8,128)(2,1)S(1)}, u32[]{:S(2)}, u32[]{:S(2)}) collective-permute-start(bf16[16,4096]{1,0:T(8,128)(2,1)S(1)} %collective-permute-done.4), channel_id=1, source_target_pairs={{0,64},{64,0},{32,96},{96,32},{128,192},{192,128},{160,224},{224,1... | collective-permute-start | bytes 393224 | tf_op jit(solution)/shard_map/ppermute | solution.py:17
  72.9 13.8 %collective-permute-start.6 = (bf16[16,4096]{1,0:T(8,128)(2,1)S(1)}, bf16[16,4096]{1,0:T(8,128)(2,1)S(1)}, u32[]{:S(2)}, u32[]{:S(2)}) collective-permute-start(bf16[16,4096]{1,0:T(8,128)(2,1)S(1)} %collective-permute-done.5), channel_id=1, source_target_pairs={{0,128},{128,0},{32,160},{160,32},{64,192},{192,64},{96,224},{224,... | collective-permute-start | bytes 393224 | tf_op jit(solution)/shard_map/ppermute | solution.py:17
  79.5 82.9 %all-to-all-start.1 = ((bf16[16,2,2048]{2,1,0:T(2,128)(2,1)}), bf16[16,2,2048]{2,1,0:T(2,128)(2,1)S(1)}, u32[]{:S(2)}, u32[]{:S(2)}) async-start(bf16[16,2,2048]{2,1,0:T(2,128)(2,1)} %reshape.98), calls=%async_computation.1 | async-start | bytes 262144 | tf_op jit(solution)/shard_map/all_to_all | solution.py:95
  86.7 8.1 %collective-permute-start.7 = (bf16[16,4096]{1,0:T(8,128)(2,1)S(1)}, bf16[16,4096]{1,0:T(8,128)(2,1)S(1)}, u32[]{:S(2)}, u32[]{:S(2)}) collective-permute-start(bf16[16,4096]{1,0:T(8,128)(2,1)S(1)} %collective-permute-done.6), channel_id=1, source_target_pairs={{0,256},{256,0},{32,288},{288,32},{64,320},{320,64},{96,352},{352,... | collective-permute-start | bytes 393224 | tf_op jit(solution)/shard_map/ppermute | solution.py:17
  124.8 21.5 %copy-start.1 = (s32[1,1,32]{2,1,0:T(1,128)S(1)}, s32[1,1,32]{2,1,0:T(1,128)}, u32[]{:S(2)}) copy-start(s32[1,1,32]{2,1,0:T(1,128)} %param.3) | copy-start | bytes 388
  162.5 137.1 %all-to-all-start = ((f32[1,32,16,4096]{3,1,0,2:T(8,128)}), f32[1,32,16,4096]{3,1,0,2:T(8,128)}, u32[]{:S(2)}, u32[]{:S(2)}) async-start(f32[1,32,16,4096]{3,1,0,2:T(8,128)} %fusion.5), calls=%async_computation | async-start | bytes 16777216 | tf_op jit(solution)/shard_map/all_to_all | solution.py:98
where the time goes:
time: 330 us; the launch traced here: 329 us
  waiting for transfers between devices  166 us (50%)
  other arithmetic  85.8 us (26%)
  starting transfers between devices  58.9 us (18%)
  matrix products  16.2 us (5%)
    all_to_all x1, waiting for transfers between devices, local(): lax.all_to_all(cost[None], 'au', split_axis=2, concat_axis=0, tiled=True)  126 us
    ppermute x8, starting transfers between devices, partner(): return lax.ppermute(block, axis, route)  43.7 us
    ppermute x8, waiting for transfers between devices, partner(): return lax.ppermute(block, axis, route)  39.2 us
    unnamed x33, other arithmetic  30.4 us
    add x1, other arithmetic, label_costs(): total = total + padded[:, :, offset:offset + width]  21.5 us
    dot_general x1, matrix products, label_costs(): jnp.einsum('ls,srw->lrw', select, total, precision=lax.Precision.HIGHEST,...  16.2 us
    broadcast_in_dim x1, other arithmetic, local(): return refine_epi(intens, depth, confidence)[None]  14.3 us
    all_to_all x1, starting transfers between devices, local(): lax.all_to_all(cost[None], 'au', split_axis=2, concat_axis=0, tiled=True)  8.06 us
  transfers between devices with their start and end apart: 10, of which 8 were waited for; matrix products, arithmetic and copies ran while one was open for 23% of the time, Pallas kernels for 0%

commit v1 on v0

v1 whole, which is shorter than its diff:
```python
import functools
import math

import jax
import jax.numpy as jnp
from jax import lax
from jax.experimental import pallas as pl
from jax.experimental.pallas import tpu as pltpu
from jax.sharding import PartitionSpec as P

MAXS = 16
RAD = 2
OFFS = 2 * MAXS + 1
CAMS = 16
ROWS = 16
TILES = 32
LANES = 128
SEG = 64
HALO = MAXS + RAD
EXT = SEG + 2 * HALO
BLOCK = 8
SCALE = math.sqrt(0.5 * math.log2(math.e))
FAR = 1e30
MESH = pl.DeviceIdType.MESH


def exchange_kernel(views, shifts, own, mir, band, flat, rows, shift_row, load_sem, zsend, zrecv, psend, precv, ready, go):
    au = lax.axis_index("au")
    vert = lax.axis_index("vert")
    facing = 30 - 2 * (vert // 2) + lax.rem(vert, 2)
    first = vert < 16

    load = pltpu.make_async_copy(views.at[0, 0], band, load_sem.at[0])
    load.start()
    load_shift = pltpu.make_async_copy(shifts.at[0], shift_row, load_sem.at[1])
    load_shift.start()

    def peer(k):
        return lax.rem(au + k, CAMS)

    def signal(sem, column, slot):
        pl.semaphore_signal(sem, inc=1, device_id={"au": column, "vert": slot}, device_id_type=MESH)

    barrier = pltpu.get_barrier_semaphore()

    @pl.when(first)
    def _():
        for k in range(CAMS):
            signal(barrier, peer(k), facing)
        for k in range(1, CAMS):
            signal(barrier, peer(k), vert)

    load.wait()
    for t in range(TILES):
        flat[pl.ds(t, ROWS, stride=TILES), :] = band[:, t * LANES : (t + 1) * LANES].astype(jnp.float32)
    for y in range(ROWS):
        rows[y, 0:TILES, :] = flat[y * TILES : (y + 1) * TILES, :].astype(jnp.bfloat16)
    load_shift.wait()
    labels = jnp.concatenate([shift_row[...].astype(jnp.float32), jnp.zeros((1, LANES - 32), jnp.float32)], axis=1)
    labels = jnp.broadcast_to(labels, (16, LANES)).astype(jnp.bfloat16)
    for y in range(ROWS):
        rows[y, TILES : TILES + 16, :] = labels

    across = [
        pltpu.make_async_remote_copy(
            src_ref=rows.at[peer(k), pl.ds(0, TILES)],
            dst_ref=mir.at[CAMS - 1 - au],
            send_sem=zsend.at[k],
            recv_sem=zrecv.at[k],
            device_id={"au": peer(k), "vert": facing},
            device_id_type=MESH,
        )
        for k in range(CAMS)
    ]
    inside = [
        pltpu.make_async_remote_copy(
            src_ref=rows.at[peer(k)],
            dst_ref=own.at[au],
            send_sem=psend.at[k],
            recv_sem=precv.at[k],
            device_id={"au": peer(k), "vert": vert},
            device_id_type=MESH,
        )
        for k in range(1, CAMS)
    ]
    keep = pltpu.make_async_copy(rows.at[au], own.at[au], load_sem.at[2])
    keep.start()

    @pl.when(first)
    def _():
        pl.semaphore_wait(barrier, CAMS - 1)
        for copy in inside:
            copy.start()
        pl.semaphore_wait(ready, CAMS)
        signal(go, au, facing)
        for copy in across:
            copy.start()

    @pl.when(jnp.logical_not(first))
    def _():
        pl.semaphore_wait(barrier, CAMS)
        for copy in across:
            copy.start()
        for k in range(CAMS):
            signal(ready, peer(k), facing)
        pl.semaphore_wait(go, 1)
        for copy in inside:
            copy.start()

    keep.wait()
    for copy in inside + across:
        copy.wait()


def exchange(views, shifts):
    return pl.pallas_call(
        exchange_kernel,
        out_shape=(
            jax.ShapeDtypeStruct((CAMS, TILES + 16, LANES), jnp.bfloat16),
            jax.ShapeDtypeStruct((CAMS, TILES, LANES), jnp.bfloat16),
        ),
        in_specs=[pl.BlockSpec(memory_space=pl.ANY)] * 2,
        out_specs=[pl.BlockSpec(memory_space=pl.ANY)] * 2,
        scratch_shapes=[
            pltpu.VMEM((ROWS, TILES * LANES), jnp.bfloat16),
            pltpu.VMEM((ROWS * TILES, LANES), jnp.float32),
            pltpu.VMEM((ROWS, TILES + 16, LANES), jnp.bfloat16),
            pltpu.VMEM((1, 32), jnp.int32),
            pltpu.SemaphoreType.DMA((3,)),
            pltpu.SemaphoreType.DMA((CAMS,)),
            pltpu.SemaphoreType.DMA((CAMS,)),
            pltpu.SemaphoreType.DMA((CAMS,)),
            pltpu.SemaphoreType.DMA((CAMS,)),
            pltpu.SemaphoreType.REGULAR,
            pltpu.SemaphoreType.REGULAR,
        ],
        compiler_params=pltpu.CompilerParams(collective_id=0, has_side_effects=True),
        name="exchange",
    )(views, shifts)


def spread(block, ref, first_row):
    for group in range(4):
        turned = block(group).T
        for half in range(2):
            ref[pl.ds(first_row * 8 + half * 4 + group, SEG, stride=8), :] = turned[half * SEG : (half + 1) * SEG]


def refine_kernel(own, mir, out, ext, facing, table, depths, costs, coh_ref, pull_ref):
    lane = lax.broadcasted_iota(jnp.int32, (8, LANES), 1)
    sub = lax.broadcasted_iota(jnp.int32, (8, LANES), 0)
    tile, member = lane % 32, lane // 32
    upper, group = sub >= 4, sub % 4
    zero = jnp.zeros((8, LANES), jnp.float32)

    def row(ref, i):
        if isinstance(i, int):
            return ref[i * 8 : i * 8 + 8, :]
        return ref[pl.ds(pl.multiple_of(i * 8, 8), 8), :]

    def put(ref, i, value):
        if isinstance(i, int):
            ref[i * 8 : i * 8 + 8, :] = value
        else:
            ref[pl.ds(pl.multiple_of(i * 8, 8), 8), :] = value

    def flat(ref, g):
        return ref[4 * g : 4 * g + 4, 0:TILES, :].astype(jnp.float32).reshape(LANES, LANES) * SCALE

    last_tile, first_tile = tile == TILES - 1, tile == 0
    for source, ref in ((own, ext), (mir, facing)):
        spread(functools.partial(flat, source), ref, HALO)
        for j in range(HALO):
            turned = pltpu.roll(row(ref, HALO + j), 4, 0)
            moved = jnp.where(last_tile, zero, pltpu.roll(turned, LANES - 1, 1))
            put(ref, HALO + SEG + j, jnp.where(upper, moved, turned))
            turned = pltpu.roll(row(ref, SEG + j), 4, 0)
            moved = jnp.where(first_tile, zero, pltpu.roll(turned, 1, 1))
            put(ref, j, jnp.where(upper, turned, moved))

    shift = own[:, TILES, :].astype(jnp.float32)
    offset = lax.broadcasted_iota(jnp.int32, (CAMS, LANES), 1).astype(jnp.float32) - MAXS
    often = jnp.zeros((CAMS, LANES), jnp.float32)
    total = jnp.zeros((CAMS, LANES), jnp.float32)
    for label in range(32):
        hit = shift[:, label : label + 1] == offset
        often = often + jnp.where(hit, 1.0, 0.0)
        total = total + jnp.where(hit, float(label), 0.0)
    both = often + pltpu.roll(total, 64, 1)

    def cams(g):
        return jnp.broadcast_to(both[4 * g : 4 * g + 4, None, :], (4, TILES, LANES)).reshape(LANES, LANES)

    for g in range(4):
        turned = cams(g).T
        for half in range(2):
            table[pl.ds(half * 4 + g, LANES, stride=8), :] = turned

    def after(value):
        a = pltpu.roll(value, LANES - 32, 1)
        b = jnp.where(group < 3, pltpu.roll(a, 7, 0), zero)
        return jnp.where(member < 3, a, b)

    def before(value):
        a = pltpu.roll(value, 32, 1)
        b = jnp.where(group > 0, pltpu.roll(a, 1, 0), zero)
        return jnp.where(member > 0, a, b)

    def boxed(values):
        pairs = [values[i] + values[i + 1] for i in range(len(values) - 1)]
        return [pairs[i] + pairs[i + 2] + values[i + 4] for i in range(len(values) - 4)]

    outside_left = jnp.logical_and(first_tile, jnp.logical_not(upper))
    outside_right = jnp.logical_and(last_tile, upper)

    def block(b, _):
        start = b * BLOCK
        left = jnp.where(jnp.logical_and(outside_left, b == 0), zero, zero + 1.0)
        right = jnp.where(jnp.logical_and(outside_right, b == SEG // BLOCK - 1), zero, zero + 1.0)

        def inside(values):
            return [v * left for v in values[:RAD]] + values[RAD:-RAD] + [v * right for v in values[-RAD:]]

        base = start + HALO - RAD
        width = BLOCK + 2 * RAD
        gx = inside([row(ext, base + i + 1) - row(ext, base + i - 1) for i in range(width)])
        gu = [after(row(ext, base + i)) - before(row(ext, base + i)) for i in range(width)]
        xx = boxed([g * g for g in gx])
        xu = boxed([g * h for g, h in zip(gx, gu)])
        unit = 0.25 / (SCALE * SCALE)
        cohs, pulls = [], []
        for i in range(BLOCK):
            jxx = (xx[i] + after(xx[i]) + before(xx[i])) * unit
            jxu = (xu[i] + after(xu[i]) + before(xu[i])) * unit
            inv = 1.0 / (jxx + 1.0)
            coh = jxx * inv
            put(coh_ref, i, coh)
            put(pull_ref, i, 4.0 * coh * (-jxu * inv))

        best = [zero + FAR for _ in range(BLOCK)]
        for s in range(OFFS):
            step = s - MAXS
            squares = []
            for i in range(width):
                d = row(ext, base + i + step) - row(facing, base + i - step)
                squares.append(d * d)
            miss = jnp.where(row(table, s) > 0.0, 0.0, FAR)
            for i, cost in enumerate(boxed(inside(squares))):
                cost = cost + miss
                put(costs, s * BLOCK + i, cost)
                best[i] = jnp.minimum(best[i], cost)
        den = [zero for _ in range(BLOCK)]
        num = [zero for _ in range(BLOCK)]
        for s in range(OFFS):
            n, m = row(table, s), row(table, 64 + s)
            for i in range(BLOCK):
                e = jnp.exp2(best[i] - row(costs, s * BLOCK + i))
                den[i] = den[i] + e * n
                num[i] = num[i] + e * m
        for i in range(BLOCK):
            conf = 1.0 / den[i]
            depth = num[i] * conf
            put(depths, start + i, (conf * depth + row(pull_ref, i)) / (conf + row(coh_ref, i)))
        return 0

    lax.fori_loop(0, SEG // BLOCK, block, 0)

    for g in range(4):
        halves = [depths[pl.ds(half * 4 + g, SEG, stride=8), :] for half in range(2)]
        out[4 * g : 4 * g + 4] = jnp.concatenate(halves, axis=0).T.reshape(4, TILES, LANES)


def refine(own, mir):
    f32 = jnp.float32
    return pl.pallas_call(
        refine_kernel,
        out_shape=jax.ShapeDtypeStruct((CAMS, TILES, LANES), f32),
        in_specs=[pl.BlockSpec(memory_space=pltpu.VMEM)] * 2,
        out_specs=pl.BlockSpec(memory_space=pltpu.VMEM),
        scratch_shapes=[
            pltpu.VMEM((EXT * 8, LANES), f32),
            pltpu.VMEM((EXT * 8, LANES), f32),
            pltpu.VMEM((LANES * 8, LANES), f32),
            pltpu.VMEM((SEG * 8, LANES), f32),
            pltpu.VMEM((OFFS * BLOCK * 8, LANES), f32),
            pltpu.VMEM((BLOCK * 8, LANES), f32),
            pltpu.VMEM((BLOCK * 8, LANES), f32),
        ],
        compiler_params=pltpu.CompilerParams(vmem_limit_bytes=32 * 1024 * 1024),
        name="refine",
    )(own, mir)


def local(views, shifts):
    own, mir = exchange(views, shifts)
    return refine(own, mir).reshape(1, CAMS, 1, TILES * LANES)


def solution(mesh):
    placed = (P("vert", "au", None, None), P("vert", "au", None))
    return jax.shard_map(
        local, mesh=mesh, in_specs=placed, out_specs=P("vert", None, "au", None), check_vma=False
    )
```

time: 330 us -> 38.4 us (0.12)
  the two profiles are of different devices: /device:TPU:27 before, /device:TPU:1 now
where the time goes in v1:
time: 38.4 us; the launch traced here: 38.2 us
  Pallas kernels  36.4 us (95%)
  local copies, waits for them, and re-layouts  1.82 us (5%)
    pallas_call x1, Pallas kernels, exchange(): pl.pallas_call(exchange_kernel, out_shape=(jax.ShapeDtypeStruct((CAMS, TI...  29.5 us
    pallas_call x1, Pallas kernels, refine(): pl.pallas_call(refine_kernel, out_shape=jax.ShapeDtypeStruct((CAMS, TILES...  6.86 us
    unnamed x4, local copies, waits for them, and re-layouts  1.82 us

profile of v1, /device:TPU:1, one launch (start us, length us, event | category | flops | bytes accessed | tf_op | source)
XLA Modules:
  0.0 38.2 jit_solution(5082121102701029954)
XLA Ops:
  0.0 29.5 %exchange.1 = (bf16[16,48,128]{2,1,0:T(8,128)(2,1)}, bf16[16,32,128]{2,1,0:T(8,128)(2,1)}) custom-call(bf16[1,1,16,4096]{3,2,1,0:T(8,128)(2,1)} %views.1, s32[1,1,32]{2,1,0:T(1,128)} %shifts.1), custom_call_target="tpu_custom_call" | custom-call | tf_op jit(solution)/shard_map/exchange/pallas_call | solution.py:116
  29.5 0.0 copy-start
  29.5 0.9 %copy-done = bf16[16,48,128]{2,1,0:T(8,128)(2,1)S(1)} copy-done((bf16[16,48,128]{2,1,0:T(8,128)(2,1)S(1)}, bf16[16,48,128]{2,1,0:T(8,128)(2,1)}, u32[]{:S(2)}) %copy-start) | copy-done | bytes 196632
  30.4 0.0 copy-start.1
  30.5 0.9 %copy-done.1 = bf16[16,32,128]{2,1,0:T(8,128)(2,1)S(1)} copy-done((bf16[16,32,128]{2,1,0:T(8,128)(2,1)S(1)}, bf16[16,32,128]{2,1,0:T(8,128)(2,1)}, u32[]{:S(2)}) %copy-start.1) | copy-done | bytes 131096
  31.4 6.9 %refine.1 = f32[16,32,128]{2,1,0:T(8,128)} custom-call(bf16[16,48,128]{2,1,0:T(8,128)(2,1)S(1)} %copy-done, bf16[16,32,128]{2,1,0:T(8,128)(2,1)S(1)} %copy-done.1), custom_call_target="tpu_custom_call" | custom-call | tf_op jit(solution)/shard_map/refine/pallas_call | solution.py:275
Async XLA Ops:
  29.5 0.9 %copy-start = (bf16[16,48,128]{2,1,0:T(8,128)(2,1)S(1)}, bf16[16,48,128]{2,1,0:T(8,128)(2,1)}, u32[]{:S(2)}) copy-start(bf16[16,48,128]{2,1,0:T(8,128)(2,1)} %get-tuple-element.7.own) | copy-start | bytes 589828
  30.4 0.9 %copy-start.1 = (bf16[16,32,128]{2,1,0:T(8,128)(2,1)S(1)}, bf16[16,32,128]{2,1,0:T(8,128)(2,1)}, u32[]{:S(2)}) copy-start(bf16[16,32,128]{2,1,0:T(8,128)(2,1)} %get-tuple-element.8.mir) | copy-start | bytes 393220

commit v2 on v1

v2 whole, which is shorter than its diff:
```python
import functools
import math

import jax
import jax.numpy as jnp
from jax import lax
from jax.experimental import pallas as pl
from jax.experimental.pallas import tpu as pltpu
from jax.sharding import PartitionSpec as P

MAXS = 16
RAD = 2
OFFS = 2 * MAXS + 1
CAMS = 16
ROWS = 16
TILES = 32
LANES = 128
SEG = 64
HALO = MAXS + RAD
EXT = SEG + 2 * HALO
BLOCK = 8
SCALE = math.sqrt(0.5 * math.log2(math.e))
FAR = 1e30
MESH = pl.DeviceIdType.MESH


def spread(block, ref, first_row):
    for group in range(4):
        turned = block(group).T
        for half in range(2):
            ref[pl.ds(first_row * 8 + half * 4 + group, SEG, stride=8), :] = turned[half * SEG : (half + 1) * SEG]


def kernel(views, shifts, out, own, mir, band, flat, rows, shift_row, ext, facing, table, depths, costs, coh_ref, pull_ref,
           load_sem, zsend, zrecv, psend, precv, ready, ready_all, go):
    au = lax.axis_index("au")
    vert = lax.axis_index("vert")
    other = 30 - 2 * (vert // 2) + lax.rem(vert, 2)
    first = vert < 16

    load = pltpu.make_async_copy(views.at[0, 0], band, load_sem.at[0])
    load.start()
    load_shift = pltpu.make_async_copy(shifts.at[0], shift_row, load_sem.at[1])
    load_shift.start()

    def peer(k):
        return lax.rem(au + k, CAMS)

    def signal(sem, column, slot):
        pl.semaphore_signal(sem, inc=1, device_id={"au": column, "vert": slot}, device_id_type=MESH)

    def each(low, high, fn):
        def body(k, _):
            fn(k)
            return 0

        lax.fori_loop(low, high, body, 0)

    def across(k):
        return pltpu.make_async_remote_copy(
            src_ref=rows.at[peer(k), pl.ds(0, TILES)],
            dst_ref=mir.at[CAMS - 1 - au],
            send_sem=zsend.at[k],
            recv_sem=zrecv.at[k],
            device_id={"au": peer(k), "vert": other},
            device_id_type=MESH,
        )

    def inside(k):
        return pltpu.make_async_remote_copy(
            src_ref=rows.at[peer(k)],
            dst_ref=own.at[au],
            send_sem=psend.at[k],
            recv_sem=precv.at[k],
            device_id={"au": peer(k), "vert": vert},
            device_id_type=MESH,
        )

    barrier = pltpu.get_barrier_semaphore()

    @pl.when(first)
    def _():
        for k in range(1, CAMS):
            signal(barrier, peer(k), vert)

    load.wait()
    for t in range(TILES):
        flat[pl.ds(t, ROWS, stride=TILES), :] = band[:, t * LANES : (t + 1) * LANES].astype(jnp.float32)
    for y in range(ROWS):
        rows[y, 0:TILES, :] = flat[y * TILES : (y + 1) * TILES, :].astype(jnp.bfloat16)

    def fill():
        load_shift.wait()
        labels = jnp.concatenate([shift_row[...].astype(jnp.float32), jnp.zeros((1, LANES - 32), jnp.float32)], axis=1)
        labels = jnp.broadcast_to(labels, (16, LANES)).astype(jnp.bfloat16)
        for y in range(ROWS):
            rows[y, TILES : TILES + 16, :] = labels

    @pl.when(first)
    def _():
        pl.semaphore_wait(barrier, CAMS - 1)
        signal(barrier, au, other)
        fill()
        each(1, CAMS, lambda k: inside(k).start())
        pl.semaphore_wait(ready, 1)
        for k in range(1, CAMS):
            signal(ready_all, peer(k), vert)
        pl.semaphore_wait(ready_all, CAMS - 1)
        signal(go, au, other)
        each(0, CAMS, lambda k: across(k).start())

    @pl.when(jnp.logical_not(first))
    def _():
        pl.semaphore_wait(barrier, 1)
        each(0, CAMS, lambda k: across(k).start())
        signal(ready, au, other)
        fill()
        pl.semaphore_wait(go, 1)
        each(1, CAMS, lambda k: inside(k).start())

    keep = pltpu.make_async_copy(rows.at[au], own.at[au], load_sem.at[2])
    keep.start()
    keep.wait()
    each(1, CAMS, lambda k: inside(k).wait_recv())

    lane = lax.broadcasted_iota(jnp.int32, (8, LANES), 1)
    sub = lax.broadcasted_iota(jnp.int32, (8, LANES), 0)
    tile, member = lane % 32, lane // 32
    upper, group = sub >= 4, sub % 4
    zero = jnp.zeros((8, LANES), jnp.float32)

    def row(ref, i):
        if isinstance(i, int):
            return ref[i * 8 : i * 8 + 8, :]
        return ref[pl.ds(pl.multiple_of(i * 8, 8), 8), :]

    def put(ref, i, value):
        if isinstance(i, int):
            ref[i * 8 : i * 8 + 8, :] = value
        else:
            ref[pl.ds(pl.multiple_of(i * 8, 8), 8), :] = value

    def flat(ref, g):
        return ref[4 * g : 4 * g + 4, 0:TILES, :].astype(jnp.float32).reshape(LANES, LANES) * SCALE

    last_tile, first_tile = tile == TILES - 1, tile == 0
    def extend(source, ref):
        spread(functools.partial(flat, source), ref, HALO)
        for j in range(HALO):
            turned = pltpu.roll(row(ref, HALO + j), 4, 0)
            moved = jnp.where(last_tile, zero, pltpu.roll(turned, LANES - 1, 1))
            put(ref, HALO + SEG + j, jnp.where(upper, moved, turned))
            turned = pltpu.roll(row(ref, SEG + j), 4, 0)
            moved = jnp.where(first_tile, zero, pltpu.roll(turned, 1, 1))
            put(ref, j, jnp.where(upper, turned, moved))

    extend(own, ext)

    shift = own[:, TILES, :].astype(jnp.float32)
    offset = lax.broadcasted_iota(jnp.int32, (CAMS, LANES), 1).astype(jnp.float32) - MAXS
    often = jnp.zeros((CAMS, LANES), jnp.float32)
    total = jnp.zeros((CAMS, LANES), jnp.float32)
    for label in range(32):
        hit = shift[:, label : label + 1] == offset
        often = often + jnp.where(hit, 1.0, 0.0)
        total = total + jnp.where(hit, float(label), 0.0)
    both = often + pltpu.roll(total, 64, 1)

    def cams(g):
        return jnp.broadcast_to(both[4 * g : 4 * g + 4, None, :], (4, TILES, LANES)).reshape(LANES, LANES)

    for g in range(4):
        turned = cams(g).T
        for half in range(2):
            table[pl.ds(half * 4 + g, LANES, stride=8), :] = turned

    def after(value):
        a = pltpu.roll(value, LANES - 32, 1)
        b = jnp.where(group < 3, pltpu.roll(a, 7, 0), zero)
        return jnp.where(member < 3, a, b)

    def before(value):
        a = pltpu.roll(value, 32, 1)
        b = jnp.where(group > 0, pltpu.roll(a, 1, 0), zero)
        return jnp.where(member > 0, a, b)

    def boxed(values):
        pairs = [values[i] + values[i + 1] for i in range(len(values) - 1)]
        return [pairs[i] + pairs[i + 2] + values[i + 4] for i in range(len(values) - 4)]

    outside_left = jnp.logical_and(first_tile, jnp.logical_not(upper))
    outside_right = jnp.logical_and(last_tile, upper)

    def epipolar(b, _):
        start = b * BLOCK
        left = jnp.where(jnp.logical_and(outside_left, b == 0), zero, zero + 1.0)
        right = jnp.where(jnp.logical_and(outside_right, b == SEG // BLOCK - 1), zero, zero + 1.0)

        def inside(values):
            return [v * left for v in values[:RAD]] + values[RAD:-RAD] + [v * right for v in values[-RAD:]]

        base = start + HALO - RAD
        width = BLOCK + 2 * RAD
        gx = inside([row(ext, base + i + 1) - row(ext, base + i - 1) for i in range(width)])
        gu = [after(row(ext, base + i)) - before(row(ext, base + i)) for i in range(width)]
        xx = boxed([g * g for g in gx])
        xu = boxed([g * h for g, h in zip(gx, gu)])
        unit = 0.25 / (SCALE * SCALE)
        cohs, pulls = [], []
        for i in range(BLOCK):
            jxx = (xx[i] + after(xx[i]) + before(xx[i])) * unit
            jxu = (xu[i] + after(xu[i]) + before(xu[i])) * unit
            inv = 1.0 / (jxx + 1.0)
            coh = jxx * inv
            put(coh_ref, start + i, coh)
            put(pull_ref, start + i, 4.0 * coh * (-jxu * inv))

        return 0

    lax.fori_loop(0, SEG // BLOCK, epipolar, 0)
    each(0, CAMS, lambda k: across(k).wait_recv())
    extend(mir, facing)

    def block(b, _):
        start = b * BLOCK
        left = jnp.where(jnp.logical_and(outside_left, b == 0), zero, zero + 1.0)
        right = jnp.where(jnp.logical_and(outside_right, b == SEG // BLOCK - 1), zero, zero + 1.0)

        def inside(values):
            return [v * left for v in values[:RAD]] + values[RAD:-RAD] + [v * right for v in values[-RAD:]]

        base = start + HALO - RAD
        width = BLOCK + 2 * RAD
        best = [zero + FAR for _ in range(BLOCK)]
        for s in range(OFFS):
            step = s - MAXS
            squares = []
            for i in range(width):
                d = row(ext, base + i + step) - row(facing, base + i - step)
                squares.append(d * d)
            miss = jnp.where(row(table, s) > 0.0, 0.0, FAR)
            for i, cost in enumerate(boxed(inside(squares))):
                cost = cost + miss
                put(costs, s * BLOCK + i, cost)
                best[i] = jnp.minimum(best[i], cost)
        den = [zero for _ in range(BLOCK)]
        num = [zero for _ in range(BLOCK)]
        for s in range(OFFS):
            n, m = row(table, s), row(table, 64 + s)
            for i in range(BLOCK):
                e = jnp.exp2(best[i] - row(costs, s * BLOCK + i))
                den[i] = den[i] + e * n
                num[i] = num[i] + e * m
        for i in range(BLOCK):
            conf = 1.0 / den[i]
            depth = num[i] * conf
            put(depths, start + i, (conf * depth + row(pull_ref, start + i)) / (conf + row(coh_ref, start + i)))
        return 0

    lax.fori_loop(0, SEG // BLOCK, block, 0)

    for g in range(4):
        halves = [depths[pl.ds(half * 4 + g, SEG, stride=8), :] for half in range(2)]
        out[4 * g : 4 * g + 4] = jnp.concatenate(halves, axis=0).T.reshape(4, TILES, LANES)

    each(0, CAMS, lambda k: across(k).wait_send())
    each(1, CAMS, lambda k: inside(k).wait_send())


def local(views, shifts):
    f32, bf16 = jnp.float32, jnp.bfloat16
    dma = pltpu.SemaphoreType.DMA
    out = pl.pallas_call(
        kernel,
        out_shape=jax.ShapeDtypeStruct((CAMS, TILES, LANES), f32),
        in_specs=[pl.BlockSpec(memory_space=pltpu.HBM)] * 2,
        out_specs=pl.BlockSpec(memory_space=pltpu.VMEM),
        scratch_shapes=[
            pltpu.VMEM((CAMS, TILES + 16, LANES), bf16),
            pltpu.VMEM((CAMS, TILES, LANES), bf16),
            pltpu.VMEM((ROWS, TILES * LANES), bf16),
            pltpu.VMEM((ROWS * TILES, LANES), f32),
            pltpu.VMEM((ROWS, TILES + 16, LANES), bf16),
            pltpu.VMEM((1, 32), jnp.int32),
            pltpu.VMEM((EXT * 8, LANES), f32),
            pltpu.VMEM((EXT * 8, LANES), f32),
            pltpu.VMEM((LANES * 8, LANES), f32),
            pltpu.VMEM((SEG * 8, LANES), f32),
            pltpu.VMEM((OFFS * BLOCK * 8, LANES), f32),
            pltpu.VMEM((SEG * 8, LANES), f32),
            pltpu.VMEM((SEG * 8, LANES), f32),
            dma((3,)),
            dma((CAMS,)),
            dma((CAMS,)),
            dma((CAMS,)),
            dma((CAMS,)),
            pltpu.SemaphoreType.REGULAR,
            pltpu.SemaphoreType.REGULAR,
            pltpu.SemaphoreType.REGULAR,
        ],
        compiler_params=pltpu.CompilerParams(
            collective_id=0, has_side_effects=True, vmem_limit_bytes=32 * 1024 * 1024
        ),
        name="light_field",
    )(*[pltpu.with_memory_space_constraint(a, pltpu.HBM) for a in (views, shifts)])
    return out.reshape(1, CAMS, 1, TILES * LANES)


def solution(mesh):
    placed = (P("vert", "au", None, None), P("vert", "au", None))
    return jax.shard_map(
        local, mesh=mesh, in_specs=placed, out_specs=P("vert", None, "au", None), check_vma=False
    )
```

time: 38.4 us -> 34.9 us (0.909)
  Pallas kernels: 36.4 us -> 34.1 us
  local copies, waits for them, and re-layouts: 1.82 us -> 0.71 us
    pallas_call x2 -> x1, Pallas kernels: 36.4 us -> 34.1 us  [local(): pl.pallas_call(kernel, out_shape=jax.ShapeDtypeStruct((CAMS, TILES, LANES...]
    unnamed x4 -> x1, local copies, waits for them, and re-layouts: 1.82 us -> 0.71 us
where the time goes in v2:
time: 34.9 us; the launch traced here: 34.8 us
  Pallas kernels  34.1 us (98%)
  local copies, waits for them, and re-layouts  0.71 us (2%)
    pallas_call x1, Pallas kernels, local(): pl.pallas_call(kernel, out_shape=jax.ShapeDtypeStruct((CAMS, TILES, LANES...  34.1 us
    unnamed x1, local copies, waits for them, and re-layouts  0.71 us

profile of v2, /device:TPU:1, one launch (start us, length us, event | category | flops | bytes accessed | tf_op | source)
XLA Modules:
  0.0 34.8 jit_solution(11402000383394037077)
XLA Ops:
  0.0 34.1 %light_field.1 = f32[16,32,128]{2,1,0:T(8,128)S(1)} custom-call(bf16[1,1,16,4096]{3,2,1,0:T(8,128)(2,1)} %views.1, s32[1,1,32]{2,1,0:T(1,128)} %shifts.1), custom_call_target="tpu_custom_call" | custom-call | tf_op jit(solution)/shard_map/light_field/pallas_call | solution.py:273
  34.1 0.7 %copy.5 = f32[1,16,1,4096]{3,2,1,0:T(1,128)} copy(f32[1,16,1,4096]{3,2,1,0:T(1,128)S(1)} %bitcast.1) | data formatting | bytes 524288

commit v3 on v2

v3 whole, which is shorter than its diff:
```python
import functools
import math

import jax
import jax.numpy as jnp
from jax import lax
from jax.experimental import pallas as pl
from jax.experimental.pallas import tpu as pltpu
from jax.sharding import PartitionSpec as P

MAXS = 16
RAD = 2
OFFS = 2 * MAXS + 1
CAMS = 16
ROWS = 16
TILES = 32
LANES = 128
SEG = 16
HALO = MAXS + RAD
EXT = SEG + 2 * HALO
SCALE = math.sqrt(0.5 * math.log2(math.e))
FAR = 1e30
MESH = pl.DeviceIdType.MESH


def kernel(views, shifts, out, own, mir, band, flat, rows, shift_row, bare, xx_ref, xu_ref, coh_ref, pull_ref, both_ref,
           turned, ext, facing, table, coh_chunk, pull_chunk, costs, result,
           load_sem, zsend, zrecv, psend, precv, ready, ready_all, go):
    au = lax.axis_index("au")
    vert = lax.axis_index("vert")
    other = 30 - 2 * (vert // 2) + lax.rem(vert, 2)
    first = vert < 16
    middle = jnp.logical_and(vert >= 6, vert < 26)
    flight = CAMS
    for slot, count in ((24, 2), (26, 8), (28, 8), (30, 6)):
        flight = jnp.where(jnp.logical_and(vert >= slot, vert < slot + 2), count, flight)

    load = pltpu.make_async_copy(views.at[0, 0], band, load_sem.at[0])
    load.start()
    load_shift = pltpu.make_async_copy(shifts.at[0], shift_row, load_sem.at[1])
    load_shift.start()

    def peer(k):
        return lax.rem(au + k, CAMS)

    def signal(sem, column, slot):
        pl.semaphore_signal(sem, inc=1, device_id={"au": column, "vert": slot}, device_id_type=MESH)

    def each(low, high, fn, unroll=None):
        def body(k, _):
            fn(k)
            return 0

        lax.fori_loop(low, high, body, 0, unroll=unroll)

    def across(k):
        return pltpu.make_async_remote_copy(
            src_ref=rows.at[peer(k), pl.ds(0, TILES)],
            dst_ref=mir.at[k],
            send_sem=zsend.at[k],
            recv_sem=zrecv.at[k],
            device_id={"au": peer(k), "vert": other},
            device_id_type=MESH,
        )

    def inside(k):
        return pltpu.make_async_remote_copy(
            src_ref=rows.at[peer(k)],
            dst_ref=own.at[au],
            send_sem=psend.at[k],
            recv_sem=precv.at[k],
            device_id={"au": peer(k), "vert": vert},
            device_id_type=MESH,
        )

    def rest(k):
        across(k - flight).wait_send()
        across(k).start()

    barrier = pltpu.get_barrier_semaphore()

    @pl.when(jnp.logical_or(first, middle))
    def _():
        for k in range(1, CAMS):
            signal(barrier, peer(k), vert)

    load.wait()
    for t in range(TILES):
        flat[pl.ds(t, ROWS, stride=TILES), :] = band[:, t * LANES : (t + 1) * LANES].astype(jnp.float32)
    for y in range(ROWS):
        rows[y, 0:TILES, :] = flat[y * TILES : (y + 1) * TILES, :].astype(jnp.bfloat16)

    def fill():
        load_shift.wait()
        labels = jnp.concatenate([shift_row[...].astype(jnp.float32), jnp.zeros((1, LANES - 32), jnp.float32)], axis=1)
        labels = jnp.broadcast_to(labels, (16, LANES)).astype(jnp.bfloat16)
        for y in range(ROWS):
            rows[y, TILES : TILES + 16, :] = labels

    @pl.when(first)
    def _():
        pl.semaphore_wait(barrier, CAMS - 1)
        signal(barrier, au, other)
        fill()
        each(1, CAMS, lambda k: inside(k).start())
        pl.semaphore_wait(ready, 1)

        @pl.when(jnp.logical_not(middle))
        def _():
            for k in range(1, CAMS):
                signal(ready_all, peer(k), vert)
            pl.semaphore_wait(ready_all, CAMS - 1)
            signal(go, au, other)

        each(0, flight, lambda k: across(k).start())

    @pl.when(jnp.logical_not(first))
    def _():
        @pl.when(middle)
        def _():
            pl.semaphore_wait(barrier, CAMS)

        @pl.when(jnp.logical_not(middle))
        def _():
            pl.semaphore_wait(barrier, 1)

        each(0, flight, lambda k: across(k).start())
        signal(ready, au, other)
        fill()

        @pl.when(jnp.logical_not(middle))
        def _():
            pl.semaphore_wait(go, 1)

        each(1, CAMS, lambda k: inside(k).start())

        each(flight, CAMS, rest)

    keep = pltpu.make_async_copy(rows.at[au], own.at[au], load_sem.at[2])
    keep.start()
    keep.wait()
    each(1, CAMS, lambda k: inside(k).wait_recv())

    blank = jnp.zeros((TILES, LANES), jnp.float32)
    wide_lane = lax.broadcasted_iota(jnp.int32, (TILES, LANES), 1)
    wide_tile = lax.broadcasted_iota(jnp.int32, (TILES, LANES), 0)

    def ahead(value, d):
        a = pltpu.roll(value, LANES - d, 1)
        b = jnp.where(wide_tile == TILES - 1, blank, pltpu.roll(a, TILES - 1, 0))
        return jnp.where(wide_lane >= LANES - d, b, a)

    def behind(value, d):
        a = pltpu.roll(value, d, 1)
        b = jnp.where(wide_tile == 0, blank, pltpu.roll(a, 1, 0))
        return jnp.where(wide_lane < d, b, a)

    def at(a):
        return pl.ds(pl.multiple_of((a + 1) * TILES, TILES), TILES)

    for ref in (bare, xx_ref, xu_ref):
        ref[0:TILES, :] = blank
        ref[(CAMS + 1) * TILES : (CAMS + 2) * TILES, :] = blank
    bare[TILES : (CAMS + 1) * TILES, :] = own[:, 0:TILES, :].astype(jnp.float32).reshape(CAMS * TILES, LANES)

    def gradients(a):
        value = bare[at(a), :]
        gx = ahead(value, 1) - behind(value, 1)
        gu = bare[at(a + 1), :] - bare[at(a - 1), :]
        xx_ref[at(a), :] = gx * gx
        xu_ref[at(a), :] = gx * gu

    each(0, CAMS, gradients, 4)

    def boxes(a):
        def box(ref):
            value = ref[at(a - 1), :] + ref[at(a), :] + ref[at(a + 1), :]
            return (behind(value, 2) + behind(value, 1) + value + ahead(value, 1) + ahead(value, 2)) * 0.25

        jxx, jxu = box(xx_ref), box(xu_ref)
        inv = 1.0 / (jxx + 1.0)
        coh = jxx * inv
        coh_ref[at(a - 1), :] = coh
        pull_ref[at(a - 1), :] = 4.0 * coh * (-jxu * inv)

    each(0, CAMS, boxes, 4)

    shift = own[:, TILES, :].astype(jnp.float32)
    offset = lax.broadcasted_iota(jnp.int32, (CAMS, LANES), 1).astype(jnp.float32) - MAXS
    often = jnp.zeros((CAMS, LANES), jnp.float32)
    total = jnp.zeros((CAMS, LANES), jnp.float32)
    for label in range(32):
        hit = shift[:, label : label + 1] == offset
        often = often + jnp.where(hit, 1.0, 0.0)
        total = total + jnp.where(hit, float(label), 0.0)
    both_ref[...] = often + pltpu.roll(total, 64, 1)

    lane = lax.broadcasted_iota(jnp.int32, (8, LANES), 1)
    sub = lax.broadcasted_iota(jnp.int32, (8, LANES), 0)
    first_tile, last_tile = lane % 32 == 0, lane % 32 == TILES - 1
    zero = jnp.zeros((8, LANES), jnp.float32)

    def right_of(value):
        a = pltpu.roll(value, 7, 0)
        b = jnp.where(last_tile, zero, pltpu.roll(a, LANES - 1, 1))
        return jnp.where(sub == 7, b, a)

    def left_of(value):
        a = pltpu.roll(value, 1, 0)
        b = jnp.where(first_tile, zero, pltpu.roll(a, 1, 1))
        return jnp.where(sub == 0, b, a)

    def camera(g, j):
        return lax.rem(2 * CAMS - 1 - au + 4 * g + j, CAMS)

    def put(ref, start, i, value):
        ref[pl.ds(pl.multiple_of((start + i) * 8, 8), 8), :] = value

    def get(ref, start, i):
        return ref[pl.ds(pl.multiple_of((start + i) * 8, 8), 8), :]

    def extend(block, ref, start):
        turned[...] = (block * SCALE).T
        values = [turned[pl.ds(i, 8, stride=SEG), :] for i in range(SEG)]
        right = [right_of(v) for v in values]
        right += [right_of(v) for v in right[:RAD]]
        left = [left_of(v) for v in values]
        left = [left_of(v) for v in left[-RAD:]] + left
        for i, value in enumerate(left + values + right):
            put(ref, start, i, value)

    def prepare(g):
        cams = [camera(g, j) for j in range(4)]

        def natural(ref):
            return jnp.concatenate([ref[pl.ds(pl.multiple_of(c * TILES, TILES), TILES), :] for c in cams], axis=0)

        block = jnp.concatenate([bare[at(c), :] for c in cams], axis=0)
        extend(block, ext, g * EXT)
        here = pl.ds(pl.multiple_of(g * LANES, LANES), LANES)
        coh_chunk[here, :] = natural(coh_ref).T
        pull_chunk[here, :] = natural(pull_ref).T
        labels = [jnp.broadcast_to(both_ref[pl.ds(c, 1), :], (TILES, LANES)) for c in cams]
        table[here, :] = jnp.concatenate(labels, axis=0).T

    each(0, 4, prepare)

    @pl.when(first)
    def _():
        each(flight, CAMS, rest)

    outside_left = jnp.where(jnp.logical_and(first_tile, sub == 0), 0.0, 1.0)
    outside_right = jnp.where(jnp.logical_and(last_tile, sub == 7), 0.0, 1.0)

    def boxed(values):
        pairs = [values[i] + values[i + 1] for i in range(len(values) - 1)]
        return [pairs[i] + pairs[i + 2] + values[i + 4] for i in range(len(values) - 4)]

    def chunk(g):
        each(0, 4, lambda j: across(4 * g + j).wait_recv())

        extend(mir[pl.ds(4 * g, 4), :, :].astype(jnp.float32).reshape(LANES, LANES), facing, 0)

        def entry(s):
            return jnp.broadcast_to(table[pl.ds(g * LANES + s, 1), :], (8, LANES))

        best = [zero + FAR for _ in range(SEG)]
        for s in range(OFFS):
            step = s - MAXS
            squares = []
            for i in range(SEG + 2 * RAD):
                d = get(ext, g * EXT, HALO - RAD + i + step) - get(facing, 0, HALO - RAD + i - step)
                squares.append(d * d)
            squares[:RAD] = [q * outside_left for q in squares[:RAD]]
            squares[-RAD:] = [q * outside_right for q in squares[-RAD:]]
            miss = jnp.where(entry(s) > 0.0, 0.0, FAR)
            for i, cost in enumerate(boxed(squares)):
                cost = cost + miss
                put(costs, s * SEG, i, cost)
                best[i] = jnp.minimum(best[i], cost)
        den = [zero for _ in range(SEG)]
        num = [zero for _ in range(SEG)]
        for s in range(OFFS):
            n, m = entry(s), entry(64 + s)
            for i in range(SEG):
                e = jnp.exp2(best[i] - get(costs, s * SEG, i))
                den[i] = den[i] + e * n
                num[i] = num[i] + e * m
        for i in range(SEG):
            here = pl.ds(g * LANES + i, 8, stride=SEG)
            conf = 1.0 / den[i]
            depth = num[i] * conf
            value = (conf * depth + pull_chunk[here, :]) / (conf + coh_chunk[here, :])
            result[pl.ds(i, 8, stride=SEG), :] = value
        back = result[...].T
        for j in range(4):
            out[camera(g, j)] = back[j * TILES : (j + 1) * TILES]

    each(0, 4, chunk)

    each(CAMS - flight, CAMS, lambda k: across(k).wait_send())
    each(1, CAMS, lambda k: inside(k).wait_send())


def local(views, shifts):
    f32, bf16 = jnp.float32, jnp.bfloat16
    dma = pltpu.SemaphoreType.DMA
    out = pl.pallas_call(
        kernel,
        out_shape=jax.ShapeDtypeStruct((CAMS, TILES, LANES), f32),
        in_specs=[pl.BlockSpec(memory_space=pltpu.HBM)] * 2,
        out_specs=pl.BlockSpec(memory_space=pltpu.VMEM),
        scratch_shapes=[
            pltpu.VMEM((CAMS, TILES + 16, LANES), bf16),
            pltpu.VMEM((CAMS, TILES, LANES), bf16),
            pltpu.VMEM((ROWS, TILES * LANES), bf16),
            pltpu.VMEM((ROWS * TILES, LANES), f32),
            pltpu.VMEM((ROWS, TILES + 16, LANES), bf16),
            pltpu.VMEM((1, 32), jnp.int32),
            pltpu.VMEM(((CAMS + 2) * TILES, LANES), f32),
            pltpu.VMEM(((CAMS + 2) * TILES, LANES), f32),
            pltpu.VMEM(((CAMS + 2) * TILES, LANES), f32),
            pltpu.VMEM((CAMS * TILES, LANES), f32),
            pltpu.VMEM((CAMS * TILES, LANES), f32),
            pltpu.VMEM((CAMS, LANES), f32),
            pltpu.VMEM((LANES, LANES), f32),
            pltpu.VMEM((4 * EXT * 8, LANES), f32),
            pltpu.VMEM((EXT * 8, LANES), f32),
            pltpu.VMEM((4 * LANES, LANES), f32),
            pltpu.VMEM((4 * LANES, LANES), f32),
            pltpu.VMEM((4 * LANES, LANES), f32),
            pltpu.VMEM((OFFS * SEG * 8, LANES), f32),
            pltpu.VMEM((LANES, LANES), f32),
            dma((3,)),
            dma((CAMS,)),
            dma((CAMS,)),
            dma((CAMS,)),
            dma((CAMS,)),
            pltpu.SemaphoreType.REGULAR,
            pltpu.SemaphoreType.REGULAR,
            pltpu.SemaphoreType.REGULAR,
        ],
        compiler_params=pltpu.CompilerParams(
            collective_id=0, has_side_effects=True, vmem_limit_bytes=32 * 1024 * 1024
        ),
        name="light_field",
    )(*[pltpu.with_memory_space_constraint(a, pltpu.HBM) for a in (views, shifts)])
    return out.reshape(1, CAMS, 1, TILES * LANES)


def solution(mesh):
    placed = (P("vert", "au", None, None), P("vert", "au", None))
    return jax.shard_map(
        local, mesh=mesh, in_specs=placed, out_specs=P("vert", None, "au", None), check_vma=False
    )
```

time: 34.9 us -> 31 us (0.89)
  Pallas kernels: 34.1 us -> 30 us
    pallas_call x1, Pallas kernels: 34.1 us -> 30 us  [local(): pl.pallas_call(kernel, out_shape=jax.ShapeDtypeStruct((CAMS, TILES, LANES...]
where the time goes in v3:
time: 31 us; the launch traced here: 30.7 us
  Pallas kernels  30 us (97%)
  local copies, waits for them, and re-layouts  0.71 us (2%)
    pallas_call x1, Pallas kernels, local(): pl.pallas_call(kernel, out_shape=jax.ShapeDtypeStruct((CAMS, TILES, LANES...  30 us
    unnamed x1, local copies, waits for them, and re-layouts  0.71 us

profile of v3, /device:TPU:1, one launch (start us, length us, event | category | flops | bytes accessed | tf_op | source)
XLA Modules:
  0.0 30.7 jit_solution(5872451927168997800)
XLA Ops:
  0.0 30.0 %light_field.1 = f32[16,32,128]{2,1,0:T(8,128)S(1)} custom-call(bf16[1,1,16,4096]{3,2,1,0:T(8,128)(2,1)} %views.1, s32[1,1,32]{2,1,0:T(1,128)} %shifts.1), custom_call_target="tpu_custom_call" | custom-call | tf_op jit(solution)/shard_map/light_field/pallas_call | solution.py:308
  30.0 0.7 %copy.5 = f32[1,16,1,4096]{3,2,1,0:T(1,128)} copy(f32[1,16,1,4096]{3,2,1,0:T(1,128)S(1)} %bitcast.1) | data formatting | bytes 524288

commit v4 on v3

--- a/solution.py
+++ b/solution.py
@@ -32,7 +32,7 @@
     first = vert < 16
     middle = jnp.logical_and(vert >= 6, vert < 26)
     flight = CAMS
-    for slot, count in ((24, 2), (26, 8), (28, 8), (30, 6)):
+    for slot, count in ((24, 3), (26, 10), (28, 8), (30, 6), (6, 8)):
         flight = jnp.where(jnp.logical_and(vert >= slot, vert < slot + 2), count, flight)
 
     load = pltpu.make_async_copy(views.at[0, 0], band, load_sem.at[0])
@@ -53,13 +53,26 @@
 
         lax.fori_loop(low, high, body, 0, unroll=unroll)
 
-    def across(k):
+    ahead_of = lax.rem(CAMS + 1 - au, CAMS)
+
+    def across(i):
+        k = jnp.where(i == 0, ahead_of, jnp.where(i <= ahead_of, i - 1, i))
         return pltpu.make_async_remote_copy(
             src_ref=rows.at[peer(k), pl.ds(0, TILES)],
             dst_ref=mir.at[k],
             send_sem=zsend.at[k],
             recv_sem=zrecv.at[k],
             device_id={"au": peer(k), "vert": other},
+            device_id_type=MESH,
+        )
+
+    def arrival(k):
+        return pltpu.make_async_remote_copy(
+            src_ref=rows.at[au, pl.ds(0, TILES)],
+            dst_ref=mir.at[k],
+            send_sem=zsend.at[k],
+            recv_sem=zrecv.at[k],
+            device_id={"au": au, "vert": other},
             device_id_type=MESH,
         )
 
@@ -124,8 +137,8 @@
         def _():
             pl.semaphore_wait(barrier, 1)
 
+        signal(ready, au, other)
         each(0, flight, lambda k: across(k).start())
-        signal(ready, au, other)
         fill()
 
         @pl.when(jnp.logical_not(middle))
@@ -253,11 +266,16 @@
     outside_right = jnp.where(jnp.logical_and(last_tile, sub == 7), 0.0, 1.0)
 
     def boxed(values):
-        pairs = [values[i] + values[i + 1] for i in range(len(values) - 1)]
-        return [pairs[i] + pairs[i + 2] + values[i + 4] for i in range(len(values) - 4)]
+        sums = []
+        for i in range(len(values) - 4):
+            if i % 8 == 0:
+                sums.append((values[i] + values[i + 1]) + (values[i + 2] + values[i + 3]) + values[i + 4])
+            else:
+                sums.append(sums[-1] + (values[i + 4] - values[i - 1]))
+        return sums
 
     def chunk(g):
-        each(0, 4, lambda j: across(4 * g + j).wait_recv())
+        each(0, 4, lambda j: arrival(4 * g + j).wait_recv())
 
         extend(mir[pl.ds(4 * g, 4), :, :].astype(jnp.float32).reshape(LANES, LANES), facing, 0)
 

time: 31 us -> 30.8 us (level)
  no operation moved by 1% of the time
where the time goes in v4:
time: 30.8 us; the launch traced here: 30.7 us
  Pallas kernels  30 us (97%)
  local copies, waits for them, and re-layouts  0.71 us (2%)
    pallas_call x1, Pallas kernels, local(): pl.pallas_call(kernel, out_shape=jax.ShapeDtypeStruct((CAMS, TILES, LANES...  30 us
    unnamed x1, local copies, waits for them, and re-layouts  0.71 us

profile of v4, /device:TPU:1, one launch (start us, length us, event | category | flops | bytes accessed | tf_op | source)
XLA Modules:
  0.0 30.7 jit_solution(7109660353444866531)
XLA Ops:
  0.0 30.0 %light_field.1 = f32[16,32,128]{2,1,0:T(8,128)S(1)} custom-call(bf16[1,1,16,4096]{3,2,1,0:T(8,128)(2,1)} %views.1, s32[1,1,32]{2,1,0:T(1,128)} %shifts.1), custom_call_target="tpu_custom_call" | custom-call | tf_op jit(solution)/shard_map/light_field/pallas_call | solution.py:326
  30.0 0.7 %copy.5 = f32[1,16,1,4096]{3,2,1,0:T(1,128)} copy(f32[1,16,1,4096]{3,2,1,0:T(1,128)S(1)} %bitcast.1) | data formatting | bytes 524288

commit v5 on v4

--- a/solution.py
+++ b/solution.py
@@ -345,8 +345,8 @@
             pltpu.VMEM((4 * EXT * 8, LANES), f32),
             pltpu.VMEM((EXT * 8, LANES), f32),
             pltpu.VMEM((4 * LANES, LANES), f32),
-            pltpu.VMEM((4 * LANES, LANES), f32),
-            pltpu.VMEM((4 * LANES, LANES), f32),
+            pltpu.VMEM((4 * LANES + SEG, LANES), f32),
+            pltpu.VMEM((4 * LANES + SEG, LANES), f32),
             pltpu.VMEM((OFFS * SEG * 8, LANES), f32),
             pltpu.VMEM((LANES, LANES), f32),
             dma((3,)),

time: 30.8 us -> 30.8 us (level)
  no operation moved by 1% of the time
where the time goes in v5:
time: 30.8 us; the launch traced here: 30.7 us
  Pallas kernels  30 us (97%)
  local copies, waits for them, and re-layouts  0.71 us (2%)
    pallas_call x1, Pallas kernels, local(): pl.pallas_call(kernel, out_shape=jax.ShapeDtypeStruct((CAMS, TILES, LANES...  30 us
    unnamed x1, local copies, waits for them, and re-layouts  0.71 us

profile of v5, /device:TPU:1, one launch (start us, length us, event | category | flops | bytes accessed | tf_op | source)
XLA Modules:
  0.0 30.7 jit_solution(11519591424524798969)
XLA Ops:
  0.0 30.0 %light_field.1 = f32[16,32,128]{2,1,0:T(8,128)S(1)} custom-call(bf16[1,1,16,4096]{3,2,1,0:T(8,128)(2,1)} %views.1, s32[1,1,32]{2,1,0:T(1,128)} %shifts.1), custom_call_target="tpu_custom_call" | custom-call | tf_op jit(solution)/shard_map/light_field/pallas_call | solution.py:326
  30.0 0.7 %copy.5 = f32[1,16,1,4096]{3,2,1,0:T(1,128)} copy(f32[1,16,1,4096]{3,2,1,0:T(1,128)S(1)} %bitcast.1) | data formatting | bytes 524288

commit v6 on v5

--- a/solution.py
+++ b/solution.py
@@ -32,7 +32,7 @@
     first = vert < 16
     middle = jnp.logical_and(vert >= 6, vert < 26)
     flight = CAMS
-    for slot, count in ((24, 3), (26, 10), (28, 8), (30, 6), (6, 8)):
+    for slot, count in ((24, 3), (26, 10), (28, 8), (30, 6), (6, 8), (4, 8)):
         flight = jnp.where(jnp.logical_and(vert >= slot, vert < slot + 2), count, flight)
 
     load = pltpu.make_async_copy(views.at[0, 0], band, load_sem.at[0])

time: 30.8 us -> 30.8 us (level)
  no operation moved by 1% of the time
where the time goes in v6:
time: 30.8 us; the launch traced here: 30.7 us
  Pallas kernels  30 us (97%)
  local copies, waits for them, and re-layouts  0.71 us (2%)
    pallas_call x1, Pallas kernels, local(): pl.pallas_call(kernel, out_shape=jax.ShapeDtypeStruct((CAMS, TILES, LANES...  30 us
    unnamed x1, local copies, waits for them, and re-layouts  0.71 us

profile of v6, /device:TPU:1, one launch (start us, length us, event | category | flops | bytes accessed | tf_op | source)
XLA Modules:
  0.0 30.7 jit_solution(14780904529250963480)
XLA Ops:
  0.0 30.0 %light_field.1 = f32[16,32,128]{2,1,0:T(8,128)S(1)} custom-call(bf16[1,1,16,4096]{3,2,1,0:T(8,128)(2,1)} %views.1, s32[1,1,32]{2,1,0:T(1,128)} %shifts.1), custom_call_target="tpu_custom_call" | custom-call | tf_op jit(solution)/shard_map/light_field/pallas_call | solution.py:326
  30.0 0.7 %copy.5 = f32[1,16,1,4096]{3,2,1,0:T(1,128)} copy(f32[1,16,1,4096]{3,2,1,0:T(1,128)S(1)} %bitcast.1) | data formatting | bytes 524288
